TPU v7x, 32 devices: a whole 2x2x4 slice. The times are simulated.
32 devices in a mesh: tm: 8 (over z, x), batch: 4 (over y, core).
Axes of the slice: x: 2, y: 2, z: 4, core: 2. Of those that a mesh axis runs over, the one named last changes fastest.
Arguments:
- state: float32 [8, 4, 256, 1152], P('tm', 'batch'), may hold values from -6 to 6
- noise_draws: bfloat16 [2, 8, 4, 256, 1152], P(None, 'tm', 'batch'), may hold values from -6 to 6
- class_vec: float32 [4, 1152], P('batch'), may hold values from -6 to 6
- window_start: int32 [4], P('batch'), may hold values from 0 to 985
- advance: int32 [4], P('batch'), may hold values from 1 to 7
- step_dt: float32 [1000], replicated, may hold values from 0.05 to 0.2
- step_sigma: float32 [1000], replicated, may hold values from 0.05 to 0.2
- w_ada: bfloat16 [1152, 3456], replicated, may hold values from -0.1875 to 0.1875
- w_up: bfloat16 [4608, 1152], P(('tm', 'batch')), may hold values from -0.1875 to 0.1875
- w_down: bfloat16 [4608, 1152], P(('tm', 'batch')), may hold values from -0.09375 to 0.09375
Outputs:
- window_out: float32 [8, 4, 256, 1152], P('tm', 'batch')
All inputs are finite; a program needn't handle non-finite values.
Results may differ from a plain program's by a relative error of at most 0.0037.
Values may be sent and summed in bfloat16 or wider, within the bound.
A program may use at most 128 MiB of HBM per device.

v0:
```python
import math

import jax
import jax.numpy as jnp
from jax import lax
from jax.sharding import PartitionSpec as P

SLIDE_BITS = 3


EPSILON = 1e-06


def spread_2(shard, axis, root):
    mine = lax.axis_index(axis) == root
    return lax.psum(jnp.where(mine, shard, jnp.zeros_like(shard)), axis)


def carried_in(part, axis, combine, identity):
    place = lax.axis_index(axis)
    gathered = lax.all_gather(part, axis)
    state = jnp.zeros_like(part) + jnp.asarray(identity, part.dtype)

    def one(turn, state):
        return combine(state, lax.dynamic_index_in_dim(gathered, turn, 0, False))

    return lax.fori_loop(0, place, one, state)


def from_behind(shard, axis, by):
    peers = lax.axis_size(axis)
    pairs = [(i, i + by) for i in range(peers) if 0 <= i + by < peers]
    return lax.ppermute(shard, axis, pairs)


def time_embed(steps_now, half_width):
    frequency = jnp.exp(-math.log(10000.0) * jnp.arange(half_width, dtype=jnp.float32) / half_width)
    angles = steps_now.astype(jnp.float32)[:, None] * frequency[None, :]
    return jnp.concatenate([jnp.cos(angles), jnp.sin(angles)], axis=1)


def dense_pair(hidden_rows, up_rows, down_rows):
    before = lax.dot_general(
        hidden_rows, up_rows, (((1,), (1,)), ((), ())), preferred_element_type=jnp.float32
    )
    activated = jax.nn.gelu(before, approximate=True).astype(jnp.bfloat16)
    return jnp.dot(activated, down_rows, preferred_element_type=jnp.float32)


def combine_sum(earlier, later):
    return earlier + later


def increment(current, noise_now, steps_now, class_vec, step_dt, step_sigma, w_ada, mlp_apply):
    images, tokens, channels = current.shape
    step_table = lax.iota(jnp.int32, step_dt.shape[0])
    onehot = (steps_now[:, None] == step_table[None, :]).astype(jnp.float32)
    step_size = jnp.sum(onehot * step_dt[None, :], axis=1)
    spread = jnp.sum(onehot * step_sigma[None, :], axis=1)
    condition = jax.nn.silu(time_embed(steps_now, channels // 2) + class_vec).astype(jnp.bfloat16)
    modulation = jnp.dot(condition, w_ada, preferred_element_type=jnp.float32)
    shift_by = modulation[:, :channels]
    scale_by = modulation[:, channels : 2 * channels]
    gate_by = modulation[:, 2 * channels :]
    mean_val = jnp.mean(current, axis=2, keepdims=True)
    centred = current - mean_val
    var_val = jnp.mean(centred * centred, axis=2, keepdims=True)
    normed = centred * lax.rsqrt(var_val + EPSILON)
    hidden_in = (normed * (1.0 + scale_by[:, None, :]) + shift_by[:, None, :]).astype(jnp.bfloat16)
    mlp_out = mlp_apply(hidden_in.reshape(images * tokens, channels)).reshape(
        images, tokens, channels
    )
    drift = gate_by[:, None, :] * mlp_out - current
    return step_size[:, None, None] * drift + spread[:, None, None] * noise_now.astype(jnp.float32)


def per_device(
    state, noise_draws, class_vec, window_start, advance, step_dt, step_sigma, w_ada, w_up, w_down
):
    window_size = lax.axis_size("tm")
    position = lax.axis_index("tm")
    up_whole, down_whole = (
        lax.all_gather(w_up, ("tm", "batch"), axis=0, tiled=True),
        lax.all_gather(w_down, ("tm", "batch"), axis=0, tiled=True),
    )

    def mlp_apply(hidden_rows):
        return dense_pair(hidden_rows, up_whole, down_whole)

    def sweep(current, noise_now, starts):
        steps_now = starts + position
        step_inc = increment(
            current, noise_now, steps_now, class_vec, step_dt, step_sigma, w_ada, mlp_apply
        )
        base_rows = spread_2(current, "tm", 0)
        prefix = carried_in(step_inc, "tm", combine_sum, jnp.zeros_like(step_inc))
        updated = base_rows + prefix
        return (updated, step_inc)

    updated, step_inc = sweep(state[0], noise_draws[0, 0], window_start)
    end_rows = updated + step_inc
    tail_rows = jnp.where(position == window_size - 1, end_rows, jnp.zeros_like(end_rows))
    moved = updated
    for section_bit in range(SLIDE_BITS):
        distance = 1 << section_bit
        arrived, arrived_tail = from_behind((moved, tail_rows), "tm", -distance)
        taken = advance >> section_bit & 1 == 1
        outside = position + distance >= window_size
        incoming = jnp.where(outside, tail_rows, arrived)
        moved = jnp.where(taken[:, None, None], incoming, moved)
        tail_rows = jnp.where(position >= window_size - distance, tail_rows, arrived_tail)
    final_rows, leftover = sweep(moved, noise_draws[1, 0], window_start + advance)
    return final_rows[None]


def solution(mesh):
    in_specs = (
        P("tm", "batch", None, None),
        P(None, "tm", "batch", None, None),
        P("batch", None),
        P("batch"),
        P("batch"),
        P(),
        P(),
        P(),
        P(("tm", "batch"), None),
        P(("tm", "batch"), None),
    )
    out_specs = P("tm", "batch", None, None)
    return jax.shard_map(
        per_device, mesh=mesh, in_specs=in_specs, out_specs=out_specs, check_vma=False
    )
```

profile of v0, /device:TPU:1, one launch (start us, length us, event | category | flops | bytes accessed | tf_op | source)
XLA Modules:
  0.0 838.0 jit_solution(11489356807884020001)
XLA Ops:
  9.4 1.4 reduce_sum.73
  11.6 4.5 fusion.73
  17.4 82.8 %all-gather.9.cloned.1.call-done = bf16[4608,1152]{1,0:T(8,128)(2,1)} async-done(((bf16[144,1152]{1,0:T(8,128)(2,1)}), bf16[4608,1152]{1,0:T(8,128)(2,1)}) %all-gather.9.cloned.1.call-update) | async-done | bytes 10616848 | tf_op jit(solution)/shard_map/all_gather | solution.py:84
  100.2 88.8 %all-gather.7.cloned.1.call-done = bf16[4608,1152]{1,0:T(8,128)(2,1)} async-done(((bf16[144,1152]{1,0:T(8,128)(2,1)}), bf16[4608,1152]{1,0:T(8,128)(2,1)}) %all-gather.7.cloned.1.call-update) | async-done | bytes 10616848 | tf_op jit(solution)/shard_map/all_gather | solution.py:83
  188.9 15.9 %fusion.18 = f32[256,1152]{1,0:T(8,128)} fusion(bf16[4608,1152]{1,0:T(8,128)(2,1)} %all-gather.9.cloned.1.call-done, f32[1,1,256,1152]{3,2,1,0:T(8,128)S(1)} %copy-done.1, bf16[4608,1152]{1,0:T(8,128)(2,1)} %all-gather.7.cloned.1.call-done, bf16[2,1,1,256,1152]{4,3,2,1,0:T(8,128)(2,1)S(1)} %copy-done.10, f32[]{:T(128)} %get-tuple-element.78, ...), kind=kOutput, calls=%fused_computation.24 | convolution fusion | flops 5449678848 | bytes 25389064 | tf_op jit(solution)/shard_map/dot_general | solution.py:47
  205.5 135.2 %all-gather.11.cloned.1.call-done = f32[2048,1152]{1,0:T(8,128)} async-done(((f32[256,1152]{1,0:T(8,128)}), f32[2048,1152]{1,0:T(8,128)}) %all-gather.11.cloned.1.call-update) | async-done | bytes 9437200 | tf_op jit(solution)/shard_map/all_gather | solution.py:21
  340.8 81.3 %all-reduce.3.cloned.1.call-done = f32[1,256,1152]{2,1,0:T(8,128)} async-done(((f32[1,256,1152]{2,1,0:T(8,128)}), f32[1,256,1152]{2,1,0:T(8,128)}) %all-reduce.3.cloned.1.call-update) | async-done | bytes 1179664 | tf_op jit(solution)/shard_map/psum | solution.py:16
  422.1 1.5 add.160
  423.6 1.3 collective-permute-start.2
  424.9 26.8 %collective-permute-done.2 = f32[1,256,1152]{2,1,0:T(8,128)S(1)} collective-permute-done((f32[1,256,1152]{2,1,0:T(8,128)S(1)}, f32[1,256,1152]{2,1,0:T(8,128)S(1)}, u32[]{:S(2)}, u32[]{:S(2)}) %collective-permute-start.2) | collective-permute-done | bytes 1179680 | tf_op jit(solution)/shard_map/ppermute | solution.py:33
  452.7 2.5 select_select_fusion.2
  456.5 1.3 collective-permute-start
  457.8 24.6 %collective-permute-done.3 = f32[1,256,1152]{2,1,0:T(8,128)S(1)} collective-permute-done((f32[1,256,1152]{2,1,0:T(8,128)S(1)}, f32[1,256,1152]{2,1,0:T(8,128)S(1)}, u32[]{:S(2)}, u32[]{:S(2)}) %collective-permute-start.3) | collective-permute-done | bytes 1179680 | tf_op jit(solution)/shard_map/ppermute | solution.py:33
  482.4 2.4 collective-permute-done
  485.8 1.9 select_select_fusion.1
  487.7 1.3 collective-permute-start.4
  489.0 1.5 collective-permute-start.1
  490.6 4.4 fusion.71
  495.7 65.0 %collective-permute-done.4 = f32[1,256,1152]{2,1,0:T(8,128)S(1)} collective-permute-done((f32[1,256,1152]{2,1,0:T(8,128)S(1)}, f32[1,256,1152]{2,1,0:T(8,128)S(1)}, u32[]{:S(2)}, u32[]{:S(2)}) %collective-permute-start.4) | collective-permute-done | bytes 1179680 | tf_op jit(solution)/shard_map/ppermute | solution.py:33
  561.6 1.9 fusion.101
  565.2 15.7 %fusion.22 = f32[1,256,1152]{2,1,0:T(8,128)} fusion(f32[1,256,1152]{2,1,0:T(8,128)S(1)} %get-tuple-element.96, bf16[4608,1152]{1,0:T(8,128)(2,1)} %all-gather.9.cloned.1.call-done, bf16[4608,1152]{1,0:T(8,128)(2,1)} %all-gather.7.cloned.1.call-done, bf16[2,1,1,256,1152]{4,3,2,1,0:T(8,128)(2,1)S(1)} %copy-done.11, f32[]{:T(128)} %get-tuple-element.77, ...), kind=kOutput, calls=%fused_computation.28 | convolution fusion | flops 5449678848 | bytes 25389064 | tf_op jit(solution)/shard_map/dot_general | solution.py:47
  581.5 165.4 %all-gather.13.cloned.1.call-done = f32[8,256,1152]{2,1,0:T(8,128)} async-done(((f32[1,256,1152]{2,1,0:T(8,128)}), f32[8,256,1152]{2,1,0:T(8,128)}) %all-gather.13.cloned.1.call-update) | async-done | bytes 9437200 | tf_op jit(solution)/shard_map/all_gather | solution.py:21
  747.1 81.7 %all-reduce.5.cloned.1.call-done = f32[1,256,1152]{2,1,0:T(8,128)} async-done(((f32[1,256,1152]{2,1,0:T(8,128)}), f32[1,256,1152]{2,1,0:T(8,128)}) %all-reduce.5.cloned.1.call-update) | async-done | bytes 1179664 | tf_op jit(solution)/shard_map/psum | solution.py:16
  828.8 2.4 add_bitcast_fusion
  (53 shorter events, 11.6 us)
Async XLA Ops:
  6.5 4.3 copy-start.8
  6.5 4.3 copy-start.9
  6.5 5.0 copy-start.6
  6.5 93.6 %all-gather.9.cloned.1.call-start = ((), (), s32[]{:S(2)}) async-start(), calls=%async_computation.2 | async-start | bytes 10948608 | tf_op jit(solution)/shard_map/all_gather | solution.py:84
  7.3 181.7 %all-gather.7.cloned.1.call-start = ((), (), s32[]{:S(2)}) async-start(), calls=%async_computation.1 | async-start | bytes 10948608 | tf_op jit(solution)/shard_map/all_gather | solution.py:83
  8.0 332.7 %all-gather.11.cloned.1.call-start = ((), (), s32[]{:S(2)}) async-start(), calls=%async_computation.4 | async-start | bytes 10616832 | tf_op jit(solution)/shard_map/all_gather | solution.py:21
  11.6 4.6 copy-start.1
  16.2 172.8 %copy-start.10 = (bf16[2,1,1,256,1152]{4,3,2,1,0:T(8,128)(2,1)S(1)}, bf16[2,1,1,256,1152]{4,3,2,1,0:T(8,128)(2,1)}, u32[]{:S(2)}) copy-start(bf16[2,1,1,256,1152]{4,3,2,1,0:T(8,128)(2,1)} %param.15) | copy-start | bytes 3538948
  204.8 217.3 %all-reduce.3.cloned.1.call-start = ((), (), s32[]{:S(2)}) async-start(), calls=%async_computation | async-start | bytes 2359296 | tf_op jit(solution)/shard_map/psum | solution.py:16
  205.4 541.5 %all-gather.13.cloned.1.call-start = ((), (), s32[]{:S(2)}) async-start(), calls=%async_computation.5 | async-start | bytes 10616832 | tf_op jit(solution)/shard_map/all_gather | solution.py:21
  422.1 30.6 %copy-start = (f32[256,1152]{1,0:T(8,128)S(1)}, f32[256,1152]{1,0:T(8,128)}, u32[]{:S(2)}) copy-start(f32[256,1152]{1,0:T(8,128)} %fusion.18) | copy-start | bytes 3538948
  423.6 28.1 %collective-permute-start.2 = (f32[1,256,1152]{2,1,0:T(8,128)S(1)}, f32[1,256,1152]{2,1,0:T(8,128)S(1)}, u32[]{:S(2)}, u32[]{:S(2)}) collective-permute-start(f32[1,256,1152]{2,1,0:T(8,128)S(1)} %add.160), channel_id=1, source_target_pairs={{4,0},{8,4},{12,8},{16,12},{20,16},{24,20},{28,24},{5,1},{9,5},{13... | collective-permute-start | bytes 3538952 | tf_op jit(solution)/shard_map/ppermute | solution.py:33
  451.7 1.0 copy-start.2
  455.2 27.2 %collective-permute-start.3 = (f32[1,256,1152]{2,1,0:T(8,128)S(1)}, f32[1,256,1152]{2,1,0:T(8,128)S(1)}, u32[]{:S(2)}, u32[]{:S(2)}) collective-permute-start(f32[1,256,1152]{2,1,0:T(8,128)S(1)} %get-tuple-element.99), channel_id=1, source_target_pairs={{8,0},{12,4},{16,8},{20,12},{24,16},{28,20},{9,1},{13,5},{17,9},{2... | collective-permute-start | bytes 3538952 | tf_op jit(solution)/shard_map/ppermute | solution.py:33
  456.5 28.3 %collective-permute-start = (f32[1,256,1152]{2,1,0:T(8,128)}, f32[1,256,1152]{2,1,0:T(8,128)S(1)}, u32[]{:S(2)}, u32[]{:S(2)}) collective-permute-start(f32[1,256,1152]{2,1,0:T(8,128)} %get-tuple-element.100), channel_id=1, source_target_pairs={{4,0},{8,4},{12,8},{16,12},{20,16},{24,20},{28,24},{5,1},{9,5},{13... | collective-permute-start | bytes 3538952 | tf_op jit(solution)/shard_map/ppermute | solution.py:33
  482.4 2.4 copy-start.4
  484.8 1.0 copy-start.5
  487.7 72.9 %collective-permute-start.4 = (f32[1,256,1152]{2,1,0:T(8,128)S(1)}, f32[1,256,1152]{2,1,0:T(8,128)S(1)}, u32[]{:S(2)}, u32[]{:S(2)}) collective-permute-start(f32[1,256,1152]{2,1,0:T(8,128)S(1)} %get-tuple-element.97), channel_id=1, source_target_pairs={{16,0},{20,4},{24,8},{28,12},{17,1},{21,5},{25,9},{29,13},{18,2},{... | collective-permute-start | bytes 3538952 | tf_op jit(solution)/shard_map/ppermute | solution.py:33
  489.0 71.6 %collective-permute-start.1 = (f32[1,256,1152]{2,1,0:T(8,128)S(1)}, f32[1,256,1152]{2,1,0:T(8,128)}, u32[]{:S(2)}, u32[]{:S(2)}) collective-permute-start(f32[1,256,1152]{2,1,0:T(8,128)S(1)} %get-tuple-element.98), channel_id=1, source_target_pairs={{8,0},{12,4},{16,8},{20,12},{24,16},{28,20},{9,1},{13,5},{17,9},{2... | collective-permute-start | bytes 3538952 | tf_op jit(solution)/shard_map/ppermute | solution.py:33
  560.6 1.0 copy-start.3
  563.6 1.2 copy-start.7
  563.6 1.6 copy-start.11
  580.9 247.8 %all-reduce.5.cloned.1.call-start = ((), (), s32[]{:S(2)}) async-start(), calls=%async_computation.3 | async-start | bytes 2359296 | tf_op jit(solution)/shard_map/psum | solution.py:16
Sparse Core Ops, SparseCore 0:
  10.3 89.8 all-gather.8
  103.1 85.8 all-gather.6
  205.0 135.6 all-gather.10
  344.0 78.0 all-reduce.2
  581.1 165.8 all-gather.12
  750.7 78.0 all-reduce.4
where the time goes:
time: 840 us; the launch traced here: 838 us
  waiting for transfers between devices  756 us (90%)
  matrix products  40.5 us (5%)
  other arithmetic  15.6 us (2%)
  between operations  15 us (2%)
    all_gather x2, waiting for transfers between devices, carried_in(): gathered = lax.all_gather(part, axis)  301 us
    psum x2, waiting for transfers between devices, spread_2(): return lax.psum(jnp.where(mine, shard, jnp.zeros_like(shard)), axis)  163 us
    ppermute x5, waiting for transfers between devices, from_behind(): return lax.ppermute(shard, axis, pairs)  119 us
    all_gather x1, waiting for transfers between devices, per_device(): lax.all_gather(w_up, ('tm', 'batch'), axis=0, tiled=True)  88.8 us
    all_gather x1, waiting for transfers between devices, per_device(): lax.all_gather(w_down, ('tm', 'batch'), axis=0, tiled=True)  82.8 us
    dot_general x2, matrix products, dense_pair(): return jnp.dot(activated, down_rows, preferred_element_type=jnp.float32)  31.6 us
  transfers between devices with their start and end apart: 11, of which 10 were waited for; matrix products, arithmetic and copies ran while one was open for 2% of the time, Pallas kernels for 0%

commit v1 on v0

--- a/solution.py
+++ b/solution.py
@@ -1,12 +1,17 @@
+import functools
 import math
 
 import jax
 import jax.numpy as jnp
 from jax import lax
+from jax.experimental import pallas as pl
+from jax.experimental.pallas import tpu as pltpu
 from jax.sharding import PartitionSpec as P
 
 SLIDE_BITS = 3
-
+MESH = pl.DeviceIdType.MESH
+WIN = 8
+LAYERS = 4
 
 EPSILON = 1e-06
 
@@ -113,6 +118,387 @@
     return final_rows[None]
 
 
+def fused(
+    start_ref, adv_ref, dt_ref, sg_ref, cls_ref, state_ref, noise_ref, wup_ref, wdn_ref, wada_ref,
+    out_ref,
+    up_full, dn_full, ada_buf, mod, a_send, a_recv, lo_send, lo_recv, cur, hid, acc, pre, o_send,
+    loc_sem, w_recv, z_sem, x_sem, y_sem, s_sem, a_ssem, a_rsem, l_ssem, l_rsem, o_ssem, o_rsem,
+):
+    tokens, width = state_ref.shape
+    part = tokens // WIN
+    depth = wup_ref.shape[0]
+    layer = 8 * depth
+    tm, bt = lax.axis_index("tm"), lax.axis_index("batch")
+    z, x = tm // 2, tm % 2
+    y, c = bt // 2, bt % 2
+    xn, yn, cn = 1 - x, 1 - y, 1 - c
+
+    def dev(zz, xx, yy, cc):
+        return (zz * 2 + xx, yy * 2 + cc)
+
+    x_dev, y_dev, s_dev = dev(z, xn, y, c), dev(z, x, yn, c), dev(z, x, y, cn)
+    up_dev, down_dev = dev(z + 1, x, y, c), dev(z - 1, x, y, c)
+
+    barrier = pltpu.get_barrier_semaphore()
+    for d in range(1, WIN):
+        pl.semaphore_signal(barrier, inc=1, device_id=((tm + d) % WIN, bt), device_id_type=MESH)
+    pl.semaphore_signal(barrier, inc=1, device_id=y_dev, device_id_type=MESH)
+    pl.semaphore_signal(barrier, inc=1, device_id=s_dev, device_id_type=MESH)
+    pl.semaphore_wait(barrier, WIN + 1)
+
+    full = (up_full, dn_full)
+    given = (wup_ref, wdn_ref)
+
+    def block(w, sid):
+        return full[w].at[pl.ds(pl.multiple_of(sid * depth, 16), depth)]
+
+    def ident(zz, xx, yy, cc):
+        return (zz * 2 + xx) * 4 + yy * 2 + cc
+
+    def send(w, sid, to, sem, own=False):
+        pltpu.make_async_remote_copy(
+            src_ref=given[w] if own else block(w, sid), dst_ref=block(w, sid),
+            send_sem=sem, recv_sem=w_recv.at[w, sid], device_id=to, device_id_type=MESH,
+        ).start()
+
+    def arrive(w, sid):
+        pltpu.make_async_remote_copy(
+            src_ref=block(w, sid), dst_ref=block(w, sid),
+            send_sem=s_sem.at[w, 0, 0], recv_sem=w_recv.at[w, sid], device_id=s_dev, device_id_type=MESH,
+        ).wait_recv()
+
+    def sent(w, sem):
+        pltpu.make_async_remote_copy(
+            src_ref=given[w], dst_ref=block(w, 0),
+            send_sem=sem, recv_sem=w_recv.at[w, 0], device_id=s_dev, device_id_type=MESH,
+        ).wait_send()
+
+    def spread(zz, own=False):
+        sid = ident(zz, x, y, c)
+        for w in (0, 1):
+            send(w, sid, x_dev, x_sem.at[w, 0, zz], own)
+            send(w, sid, y_dev, y_sem.at[w, 0, zz], own)
+        for w in (0, 1):
+            send(w, sid, s_dev, s_sem.at[w, 0, zz], own)
+
+    def side(zz):
+        from_x, from_y = ident(zz, xn, y, c), ident(zz, x, yn, c)
+        arrive(0, from_x)
+        send(0, from_x, y_dev, y_sem.at[0, 1, zz])
+        arrive(1, from_y)
+        send(1, from_y, x_dev, x_sem.at[1, 1, zz])
+        arrive(1, from_x)
+        arrive(0, from_y)
+        for w in (0, 1):
+            send(w, from_x, s_dev, s_sem.at[w, 1, zz])
+            send(w, from_y, s_dev, s_sem.at[w, 2, zz])
+
+    me = ident(z, x, y, c)
+
+    @pl.when(z < LAYERS - 1)
+    def _():
+        for w in (0, 1):
+            send(w, me, up_dev, z_sem.at[w, 0, z], True)
+
+    @pl.when(z > 0)
+    def _():
+        for w in (0, 1):
+            send(w, me, down_dev, z_sem.at[w, 1, z], True)
+
+    spread(z, True)
+    local = [
+        pltpu.make_async_copy(wada_ref, ada_buf, loc_sem.at[0]),
+        pltpu.make_async_copy(wup_ref, block(0, me), loc_sem.at[1]),
+        pltpu.make_async_copy(wdn_ref, block(1, me), loc_sem.at[2]),
+    ]
+    for copy in local:
+        copy.start()
+
+    for t in range(WIN):
+        rows = pl.ds(t * part, part)
+        whole = state_ref[rows, :]
+        high = whole.astype(jnp.bfloat16)
+        a_send[t, 0:part, :] = high
+        lo_send[t] = (whole - high.astype(jnp.float32)).astype(jnp.bfloat16)
+        a_send[t, part : 2 * part, :] = noise_ref[0, rows, :]
+        a_send[t, 2 * part : 3 * part, :] = noise_ref[1, rows, :]
+    a_recv[tm] = a_send[tm]
+
+    start, adv = start_ref[0], adv_ref[0]
+    row = lax.broadcasted_iota(jnp.int32, (2 * WIN, width), 0)
+    lane = lax.broadcasted_iota(jnp.int32, (2 * WIN, width), 1)
+    half = width // 2
+    late = row >= WIN
+    steps = (start + jnp.where(late, adv + row - WIN, row)).astype(jnp.float32)
+    turn = jnp.where(lane >= half, lane - half, lane).astype(jnp.float32)
+    angles = steps * jnp.exp(-math.log(10000.0) * turn / half)
+    embed = jnp.where(lane >= half, jnp.sin(angles), jnp.cos(angles))
+    condition = jax.nn.silu(embed + cls_ref[...]).astype(jnp.bfloat16)
+    for copy in local:
+        copy.wait()
+    for third in range(3):
+        columns = slice(third * width, (third + 1) * width)
+        mod[:, columns] = jnp.dot(condition, ada_buf[:, columns], preferred_element_type=jnp.float32)
+
+    def a_copy(d):
+        to = (tm + d) % WIN
+        return pltpu.make_async_remote_copy(
+            src_ref=a_send.at[to], dst_ref=a_recv.at[tm], send_sem=a_ssem.at[d],
+            recv_sem=a_rsem.at[tm], device_id=(to, bt), device_id_type=MESH,
+        )
+
+    def l_copy(d):
+        return pltpu.make_async_remote_copy(
+            src_ref=lo_send.at[d], dst_ref=lo_recv, send_sem=l_ssem.at[d],
+            recv_sem=l_rsem, device_id=(d, bt), device_id_type=MESH,
+        )
+
+    def round_z(r):
+        @pl.when(z >= r)
+        def _():
+            zz = z - r
+            sid = ident(zz, x, y, c)
+            for w in (0, 1):
+                arrive(w, sid)
+
+                @pl.when(z < LAYERS - 1)
+                def _():
+                    send(w, sid, up_dev, z_sem.at[w, 0, zz])
+
+            spread(zz)
+
+        @pl.when(z + r < LAYERS)
+        def _():
+            zz = z + r
+            sid = ident(zz, x, y, c)
+            for w in (0, 1):
+                arrive(w, sid)
+
+                @pl.when(z > 0)
+                def _():
+                    send(w, sid, down_dev, z_sem.at[w, 1, zz])
+
+            spread(zz)
+
+    def round_side(r):
+        if r == 0:
+            side(z)
+            return
+
+        @pl.when(z >= r)
+        def _():
+            side(z - r)
+
+        @pl.when(z + r < LAYERS)
+        def _():
+            side(z + r)
+
+    round_z(1)
+    round_side(0)
+    round_z(2)
+    for d in range(1, WIN):
+        a_copy(d).start()
+
+    @pl.when(tm == 0)
+    def _():
+        lo_recv[...] = lo_send[0]
+        for d in range(1, WIN):
+            l_copy(d).start()
+
+    round_side(1)
+    round_z(3)
+    round_side(2)
+    round_side(3)
+
+    def a_arrive(d):
+        src = (tm + d) % WIN
+        pltpu.make_async_remote_copy(
+            src_ref=a_send.at[src], dst_ref=a_recv.at[src], send_sem=a_ssem.at[d],
+            recv_sem=a_rsem.at[src], device_id=(src, bt), device_id_type=MESH,
+        ).wait_recv()
+
+    for d in range(1, WIN):
+        a_arrive(d)
+
+    @pl.when(tm > 0)
+    def _():
+        l_copy(1).wait_recv()
+
+    for j in range(WIN):
+        cur[j] = a_recv[j, 0:part, :].astype(jnp.float32)
+
+    def before_mlp(s):
+        @pl.loop(0, WIN)
+        def _(j):
+            now = cur[j]
+            centred = now - jnp.mean(now, axis=1, keepdims=True)
+            var = jnp.mean(centred * centred, axis=1, keepdims=True)
+            normed = centred * lax.rsqrt(var + EPSILON)
+            shift = mod[pl.ds(s * WIN + j, 1), 0:width]
+            scale = mod[pl.ds(s * WIN + j, 1), width : 2 * width]
+            rows = pl.ds(pl.multiple_of(j * part, part), part)
+            hid[rows, :] = (normed * (1.0 + scale) + shift).astype(jnp.bfloat16)
+            acc[rows, :] = jnp.zeros((part, width), jnp.float32)
+
+    def mlp(first, count):
+        rows = pl.ds(pl.multiple_of(first, 128), count)
+        before = lax.dot_general(
+            hid[...], up_full[rows, :], (((1,), (1,)), ((), ())), preferred_element_type=jnp.float32
+        )
+        act = jax.nn.gelu(before, approximate=True).astype(jnp.bfloat16)
+        acc[...] += jnp.dot(act, dn_full[rows, :], preferred_element_type=jnp.float32)
+
+    def after_mlp(s, base):
+        pre[0] = base
+        for j in range(WIN):
+            k = start + s * adv + j
+            rows = pl.ds(j * part, part)
+            gate = mod[s * WIN + j : s * WIN + j + 1, 2 * width : 3 * width]
+            noise = a_recv[j, (1 + s) * part : (2 + s) * part, :].astype(jnp.float32)
+            pre[j + 1] = pre[j] + (dt_ref[k] * (gate * acc[rows, :] - cur[j]) + sg_ref[k] * noise)
+
+    before_mlp(0)
+    flip = z // 2
+    near = z + flip * (3 - 2 * z)
+
+    @pl.loop(0, LAYERS)
+    def _(p):
+        early = 1 - p // 2
+        order = p + near * early * (1 - 2 * p)
+        zz = order + flip * (3 - 2 * order)
+        across = ident(zz, xn, yn, c)
+        for w in (0, 1):
+            arrive(w, across)
+            send(w, across, s_dev, s_sem.at[w, 3, zz])
+        for xx in (0, 1):
+            for yy in (0, 1):
+                for w in (0, 1):
+                    arrive(w, ident(zz, xx, yy, cn))
+
+        @pl.loop(0, 3)
+        def _(i):
+            mlp(zz * layer + i * (layer // 3), layer // 3)
+
+    after_mlp(0, cur[0] + lo_recv[...].astype(jnp.float32))
+    for j in range(WIN):
+        cur[j] = pre[jnp.minimum(adv + j, WIN)]
+    before_mlp(1)
+
+    @pl.loop(0, 3)
+    def _(i):
+        for k in range(3):
+            mlp((i * 3 + k) * (LAYERS * layer // 9), LAYERS * layer // 9)
+
+    after_mlp(1, cur[0])
+    for j in range(WIN):
+        o_send[j] = pre[j].astype(jnp.bfloat16)
+
+    own_rows = pl.ds(pl.multiple_of(tm * part, part), part)
+
+    def o_copy(d):
+        to = (tm + d) % WIN
+        return pltpu.make_async_remote_copy(
+            src_ref=o_send.at[to], dst_ref=out_ref.at[own_rows], send_sem=o_ssem.at[d],
+            recv_sem=o_rsem.at[tm], device_id=(to, bt), device_id_type=MESH,
+        )
+
+    def o_arrive(d):
+        src = (tm + d) % WIN
+        pltpu.make_async_remote_copy(
+            src_ref=o_send.at[src],
+            dst_ref=out_ref.at[pl.ds(pl.multiple_of(src * part, part), part)],
+            send_sem=o_ssem.at[d], recv_sem=o_rsem.at[src], device_id=(src, bt), device_id_type=MESH,
+        ).wait_recv()
+
+    for d in range(1, WIN):
+        o_copy(d).start()
+    mine = pltpu.make_async_copy(o_send.at[tm], out_ref.at[own_rows], loc_sem.at[0])
+    mine.start()
+
+    for zz in range(LAYERS):
+        for w in (0, 1):
+            @pl.when((z < LAYERS - 1) & (zz <= z))
+            def _():
+                sent(w, z_sem.at[w, 0, zz])
+
+            @pl.when((z > 0) & (zz >= z))
+            def _():
+                sent(w, z_sem.at[w, 1, zz])
+
+            sent(w, x_sem.at[w, 0, zz])
+            sent(w, y_sem.at[w, 0, zz])
+            for kind in range(4):
+                sent(w, s_sem.at[w, kind, zz])
+        sent(0, y_sem.at[0, 1, zz])
+        sent(1, x_sem.at[1, 1, zz])
+    for d in range(1, WIN):
+        a_copy(d).wait_send()
+
+    @pl.when(tm == 0)
+    def _():
+        for d in range(1, WIN):
+            l_copy(d).wait_send()
+
+    mine.wait()
+    for d in range(1, WIN):
+        o_arrive(d)
+        o_copy(d).wait_send()
+
+
+def per_device_fused(
+    state, noise_draws, class_vec, window_start, advance, step_dt, step_sigma, w_ada, w_up, w_down
+):
+    tokens, width = state.shape[2:]
+    hidden = w_up.shape[0] * WIN * 4
+    part = tokens // WIN
+    bf16, f32 = jnp.bfloat16, jnp.float32
+    vmem, smem = pl.BlockSpec(memory_space=pltpu.VMEM), pl.BlockSpec(memory_space=pltpu.SMEM)
+    dma = pltpu.SemaphoreType.DMA
+    flops = 2 * 2 * 2 * tokens * width * hidden
+    out = pl.pallas_call(
+        fused,
+        out_shape=jax.ShapeDtypeStruct((tokens, width), bf16),
+        in_specs=[smem] * 4 + [vmem] * 5 + [pl.BlockSpec(memory_space=pl.ANY)],
+        out_specs=pl.BlockSpec(memory_space=pl.ANY),
+        scratch_shapes=[
+            pltpu.VMEM((hidden, width), bf16),
+            pltpu.VMEM((hidden, width), bf16),
+            pltpu.VMEM(w_ada.shape, bf16),
+            pltpu.VMEM((2 * WIN, 3 * width), f32),
+            pltpu.VMEM((WIN, 3 * part, width), bf16),
+            pltpu.VMEM((WIN, 3 * part, width), bf16),
+            pltpu.VMEM((WIN, part, width), bf16),
+            pltpu.VMEM((part, width), bf16),
+            pltpu.VMEM((WIN, part, width), f32),
+            pltpu.VMEM((tokens, width), bf16),
+            pltpu.VMEM((tokens, width), f32),
+            pltpu.VMEM((WIN + 1, part, width), f32),
+            pltpu.VMEM((WIN, part, width), bf16),
+            dma((3,)),
+            dma((2, 32)),
+            dma((2, 2, LAYERS)),
+            dma((2, 2, LAYERS)),
+            dma((2, 2, LAYERS)),
+            dma((2, 4, LAYERS)),
+            dma((WIN,)),
+            dma((WIN,)),
+            dma((WIN,)),
+            dma,
+            dma((WIN,)),
+            dma((WIN,)),
+        ],
+        compiler_params=pltpu.CompilerParams(
+            collective_id=0, has_side_effects=True, vmem_limit_bytes=58 * 2**20
+        ),
+        cost_estimate=pl.CostEstimate(flops=flops, bytes_accessed=2 * w_ada.size, transcendentals=0),
+        name="picard",
+    )(
+        window_start, advance, step_dt, step_sigma, class_vec,
+        state[0, 0], noise_draws[:, 0, 0], w_up, w_down, w_ada,
+    )
+    return out.astype(f32)[None, None]
+
+
 def solution(mesh):
     in_specs = (
         P("tm", "batch", None, None),
@@ -127,6 +513,8 @@
         P(("tm", "batch"), None),
     )
     out_specs = P("tm", "batch", None, None)
+    small = mesh.shape["tm"] == WIN and mesh.shape["batch"] == 4
     return jax.shard_map(
-        per_device, mesh=mesh, in_specs=in_specs, out_specs=out_specs, check_vma=False
+        per_device_fused if small else per_device,
+        mesh=mesh, in_specs=in_specs, out_specs=out_specs, check_vma=False,
     )

time: 840 us -> 153 us (0.18)
  waiting for transfers between devices: 756 us -> 0 us
  Pallas kernels: 0 us -> 147 us
  matrix products: 40.5 us -> 0 us
  between operations: 15 us -> 1.3 us
  other arithmetic: 15.6 us -> 2.15 us
    all_gather x4 -> x0, waiting for transfers between devices: 472 us -> none  [the longest x2 301 us: carried_in(): gathered = lax.all_gather(part, axis)]
    psum x2 -> x0, waiting for transfers between devices: 163 us -> none  [spread_2(): return lax.psum(jnp.where(mine, shard, jnp.zeros_like(shard)), axis)]
    pallas_call x0 -> x1, Pallas kernels: none -> 147 us  [per_device_fused(): pl.pallas_call(fused, out_shape=jax.ShapeDtypeStruct((tokens, width), bf1...]
    ppermute x5 -> x0, waiting for transfers between devices: 119 us -> none  [from_behind(): return lax.ppermute(shard, axis, pairs)]
    dot_general x4 -> x0, matrix products: 40.5 us -> none  [the longest x2 31.6 us: dense_pair(): return jnp.dot(activated, down_rows, preferred_element_type=jnp.float32)]
  transfers between devices with their start and end apart: 11 -> 0, of which waited for: 10 -> 0; matrix products, arithmetic and copies ran while one was open for 2% -> 0% of each run, Pallas kernels for 0% -> 0%
where the time goes in v1:
time: 153 us; the launch traced here: 150 us
  Pallas kernels  147 us (96%)
  other arithmetic  2.15 us (1%)
    pallas_call x1, Pallas kernels, per_device_fused(): pl.pallas_call(fused, out_shape=jax.ShapeDtypeStruct((tokens, width), bf1...  147 us

profile of v1, /device:TPU:1, one launch (start us, length us, event | category | flops | bytes accessed | tf_op | source)
XLA Modules:
  0.0 150.2 jit_solution(7435009345598931617)
XLA Ops:
  1.3 146.7 %picard.1 = bf16[256,1152]{1,0:T(8,128)(2,1)} custom-call(s32[1]{0:T(128)S(6)} %copy.11.start_ref, s32[1]{0:T(128)S(6)} %copy.12.adv_ref, f32[1000]{0:T(1024)} %dt_ref.1, f32[1000]{0:T(1024)} %sg_ref.1, f32[1,1152]{1,0:T(1,128)} %cls_ref.1, f32[256,1152]{1,0:T(8,128)} %bitcast.5, bf16[2,256,1152]{2,1,0:T(8,128)(2,1)} %bitcast.6, bf16[144,1152]{1,0:T(8,128)(2,1)} %wup_ref.1, ...), custom_call_target="tpu_custom_call" | custom-call | flops 10871635968 | bytes 7962624 | tf_op jit(solution)/shard_map/picard/pallas_call | solution.py:458
  148.0 2.2 %bitcast_convert_fusion = f32[1,1,256,1152]{3,2,1,0:T(8,128)} fusion(bf16[256,1152]{1,0:T(8,128)(2,1)} %picard.1), kind=kLoop, calls=%fused_computation | loop fusion | flops 294912 | bytes 1769472 | tf_op jit(solution)/shard_map/broadcast_in_dim | solution.py:499

commit v2 on v1

--- a/solution.py
+++ b/solution.py
@@ -118,11 +118,15 @@
     return final_rows[None]
 
 
+SPLIT = (0, 2, 6, 9)
+TURNED = 2
+
+
 def fused(
     start_ref, adv_ref, dt_ref, sg_ref, cls_ref, state_ref, noise_ref, wup_ref, wdn_ref, wada_ref,
     out_ref,
-    up_full, dn_full, ada_buf, mod, a_send, a_recv, lo_send, lo_recv, cur, hid, acc, pre, o_send,
-    loc_sem, w_recv, z_sem, x_sem, y_sem, s_sem, a_ssem, a_rsem, l_ssem, l_rsem, o_ssem, o_rsem,
+    up_full, dn_full, ada_buf, mod, a_send, a_recv, lo_send, lo_recv, cur, hid, acc, pre, o_send, act_all,
+    loc_sem, w_recv, z_sem, x_sem, y_sem, s_sem, a_ssem, a_rsem, n_ssem, n_rsem, l_ssem, l_rsem, o_ssem, o_rsem,
 ):
     tokens, width = state_ref.shape
     part = tokens // WIN
@@ -167,6 +171,18 @@
             send_sem=s_sem.at[w, 0, 0], recv_sem=w_recv.at[w, sid], device_id=s_dev, device_id_type=MESH,
         ).wait_recv()
 
+    turned = depth * TURNED // 9 // 16 * 16
+    cuts = ((0, turned), (turned, depth - turned))
+
+    def piece(k, sid):
+        return dn_full.at[pl.ds(pl.multiple_of(sid * depth + cuts[k][0], 16), cuts[k][1])]
+
+    def piece_copy(k, sid, to, sem):
+        return pltpu.make_async_remote_copy(
+            src_ref=piece(k, sid), dst_ref=piece(k, sid),
+            send_sem=sem, recv_sem=w_recv.at[1 + k, sid], device_id=to, device_id_type=MESH,
+        )
+
     def sent(w, sem):
         pltpu.make_async_remote_copy(
             src_ref=given[w], dst_ref=block(w, 0),
@@ -186,8 +202,9 @@
         arrive(0, from_x)
         send(0, from_x, y_dev, y_sem.at[0, 1, zz])
         arrive(1, from_y)
-        send(1, from_y, x_dev, x_sem.at[1, 1, zz])
+        piece_copy(1, from_y, x_dev, x_sem.at[1, 1, zz]).start()
         arrive(1, from_x)
+        piece_copy(0, from_x, y_dev, y_sem.at[1, 1, zz]).start()
         arrive(0, from_y)
         for w in (0, 1):
             send(w, from_x, s_dev, s_sem.at[w, 1, zz])
@@ -240,11 +257,20 @@
         columns = slice(third * width, (third + 1) * width)
         mod[:, columns] = jnp.dot(condition, ada_buf[:, columns], preferred_element_type=jnp.float32)
 
+    first, second = pl.ds(0, 2 * part), pl.ds(2 * part, part)
+
     def a_copy(d):
         to = (tm + d) % WIN
         return pltpu.make_async_remote_copy(
-            src_ref=a_send.at[to], dst_ref=a_recv.at[tm], send_sem=a_ssem.at[d],
+            src_ref=a_send.at[to, first], dst_ref=a_recv.at[tm, first], send_sem=a_ssem.at[d],
             recv_sem=a_rsem.at[tm], device_id=(to, bt), device_id_type=MESH,
+        )
+
+    def n_copy(d):
+        to = (tm + d) % WIN
+        return pltpu.make_async_remote_copy(
+            src_ref=a_send.at[to, second], dst_ref=a_recv.at[tm, second], send_sem=n_ssem.at[d],
+            recv_sem=n_rsem.at[tm], device_id=(to, bt), device_id_type=MESH,
         )
 
     def l_copy(d):
@@ -309,12 +335,21 @@
     round_z(3)
     round_side(2)
     round_side(3)
+    for d in range(1, WIN):
+        n_copy(d).start()
 
     def a_arrive(d):
         src = (tm + d) % WIN
         pltpu.make_async_remote_copy(
-            src_ref=a_send.at[src], dst_ref=a_recv.at[src], send_sem=a_ssem.at[d],
+            src_ref=a_send.at[src, first], dst_ref=a_recv.at[src, first], send_sem=a_ssem.at[d],
             recv_sem=a_rsem.at[src], device_id=(src, bt), device_id_type=MESH,
+        ).wait_recv()
+
+    def n_arrive(d):
+        src = (tm + d) % WIN
+        pltpu.make_async_remote_copy(
+            src_ref=a_send.at[src, second], dst_ref=a_recv.at[src, second], send_sem=n_ssem.at[d],
+            recv_sem=n_rsem.at[src], device_id=(src, bt), device_id_type=MESH,
         ).wait_recv()
 
     for d in range(1, WIN):
@@ -348,13 +383,13 @@
         act = jax.nn.gelu(before, approximate=True).astype(jnp.bfloat16)
         acc[...] += jnp.dot(act, dn_full[rows, :], preferred_element_type=jnp.float32)
 
-    def after_mlp(s, base):
+    def after_mlp(base):
         pre[0] = base
         for j in range(WIN):
-            k = start + s * adv + j
+            k = start + j
             rows = pl.ds(j * part, part)
-            gate = mod[s * WIN + j : s * WIN + j + 1, 2 * width : 3 * width]
-            noise = a_recv[j, (1 + s) * part : (2 + s) * part, :].astype(jnp.float32)
+            gate = mod[j : j + 1, 2 * width : 3 * width]
+            noise = a_recv[j, part : 2 * part, :].astype(jnp.float32)
             pre[j + 1] = pre[j] + (dt_ref[k] * (gate * acc[rows, :] - cur[j]) + sg_ref[k] * noise)
 
     before_mlp(0)
@@ -367,8 +402,10 @@
         order = p + near * early * (1 - 2 * p)
         zz = order + flip * (3 - 2 * order)
         across = ident(zz, xn, yn, c)
-        for w in (0, 1):
-            arrive(w, across)
+        arrive(0, across)
+        for k in (0, 1):
+            piece_copy(k, across, s_dev, s_sem.at[1, 3, zz]).wait_recv()
+        for w in (0, 1):
             send(w, across, s_dev, s_sem.at[w, 3, zz])
         for xx in (0, 1):
             for yy in (0, 1):
@@ -379,39 +416,60 @@
         def _(i):
             mlp(zz * layer + i * (layer // 3), layer // 3)
 
-    after_mlp(0, cur[0] + lo_recv[...].astype(jnp.float32))
+    after_mlp(cur[0] + lo_recv[...].astype(jnp.float32))
     for j in range(WIN):
         cur[j] = pre[jnp.minimum(adv + j, WIN)]
     before_mlp(1)
+    rows_used = (WIN - 1) * part
+    hidden = LAYERS * layer
 
     @pl.loop(0, 3)
     def _(i):
         for k in range(3):
-            mlp((i * 3 + k) * (LAYERS * layer // 9), LAYERS * layer // 9)
-
-    after_mlp(1, cur[0])
-    for j in range(WIN):
-        o_send[j] = pre[j].astype(jnp.bfloat16)
+            rows = pl.ds(pl.multiple_of((i * 3 + k) * (hidden // 9), 128), hidden // 9)
+            before = lax.dot_general(
+                hid[0:rows_used, :], up_full[rows, :], (((1,), (1,)), ((), ())),
+                preferred_element_type=jnp.float32,
+            )
+            act_all[:, rows] = jax.nn.gelu(before, approximate=True).astype(jnp.bfloat16)
 
     own_rows = pl.ds(pl.multiple_of(tm * part, part), part)
 
-    def o_copy(d):
+    def o_copy(b, d):
         to = (tm + d) % WIN
         return pltpu.make_async_remote_copy(
-            src_ref=o_send.at[to], dst_ref=out_ref.at[own_rows], send_sem=o_ssem.at[d],
-            recv_sem=o_rsem.at[tm], device_id=(to, bt), device_id_type=MESH,
-        )
-
-    def o_arrive(d):
+            src_ref=o_send.at[to, :, spans[b]], dst_ref=out_ref.at[own_rows, spans[b]],
+            send_sem=o_ssem.at[b, d], recv_sem=o_rsem.at[b, tm],
+            device_id=(to, bt), device_id_type=MESH,
+        )
+
+    def o_arrive(b, d):
         src = (tm + d) % WIN
         pltpu.make_async_remote_copy(
-            src_ref=o_send.at[src],
-            dst_ref=out_ref.at[pl.ds(pl.multiple_of(src * part, part), part)],
-            send_sem=o_ssem.at[d], recv_sem=o_rsem.at[src], device_id=(src, bt), device_id_type=MESH,
+            src_ref=o_send.at[src, :, spans[b]],
+            dst_ref=out_ref.at[pl.ds(pl.multiple_of(src * part, part), part), spans[b]],
+            send_sem=o_ssem.at[b, d], recv_sem=o_rsem.at[b, src],
+            device_id=(src, bt), device_id_type=MESH,
         ).wait_recv()
 
     for d in range(1, WIN):
-        o_copy(d).start()
+        n_arrive(d)
+    edges = tuple(width * e // 9 for e in SPLIT)
+    spans = tuple(pl.ds(lo, hi - lo) for lo, hi in zip(edges, edges[1:]))
+    for b, (lo, hi) in enumerate(zip(edges, edges[1:])):
+        mlp_out = jnp.dot(act_all[...], dn_full[:, lo:hi], preferred_element_type=jnp.float32)
+        total = cur[0, :, lo:hi]
+        for j in range(WIN):
+            o_send[j, :, lo:hi] = total.astype(jnp.bfloat16)
+            if j == WIN - 1:
+                break
+            k = start + adv + j
+            gate = mod[WIN + j : WIN + j + 1, 2 * width + lo : 2 * width + hi]
+            noise = a_recv[j, 2 * part : 3 * part, lo:hi].astype(jnp.float32)
+            drift = gate * mlp_out[j * part : (j + 1) * part] - cur[j, :, lo:hi]
+            total = total + (dt_ref[k] * drift + sg_ref[k] * noise)
+        for d in range(1, WIN):
+            o_copy(b, d).start()
     mine = pltpu.make_async_copy(o_send.at[tm], out_ref.at[own_rows], loc_sem.at[0])
     mine.start()
 
@@ -430,9 +488,11 @@
             for kind in range(4):
                 sent(w, s_sem.at[w, kind, zz])
         sent(0, y_sem.at[0, 1, zz])
-        sent(1, x_sem.at[1, 1, zz])
+        piece_copy(1, 0, s_dev, x_sem.at[1, 1, zz]).wait_send()
+        piece_copy(0, 0, s_dev, y_sem.at[1, 1, zz]).wait_send()
     for d in range(1, WIN):
         a_copy(d).wait_send()
+        n_copy(d).wait_send()
 
     @pl.when(tm == 0)
     def _():
@@ -440,9 +500,10 @@
             l_copy(d).wait_send()
 
     mine.wait()
-    for d in range(1, WIN):
-        o_arrive(d)
-        o_copy(d).wait_send()
+    for b in range(len(spans)):
+        for d in range(1, WIN):
+            o_arrive(b, d)
+            o_copy(b, d).wait_send()
 
 
 def per_device_fused(
@@ -474,8 +535,9 @@
             pltpu.VMEM((tokens, width), f32),
             pltpu.VMEM((WIN + 1, part, width), f32),
             pltpu.VMEM((WIN, part, width), bf16),
+            pltpu.VMEM(((WIN - 1) * part, hidden), bf16),
             dma((3,)),
-            dma((2, 32)),
+            dma((3, 32)),
             dma((2, 2, LAYERS)),
             dma((2, 2, LAYERS)),
             dma((2, 2, LAYERS)),
@@ -483,9 +545,11 @@
             dma((WIN,)),
             dma((WIN,)),
             dma((WIN,)),
-            dma,
             dma((WIN,)),
             dma((WIN,)),
+            dma,
+            dma((len(SPLIT) - 1, WIN)),
+            dma((len(SPLIT) - 1, WIN)),
         ],
         compiler_params=pltpu.CompilerParams(
             collective_id=0, has_side_effects=True, vmem_limit_bytes=58 * 2**20

time: 153 us -> 146 us (0.954); the launches traced: 150 us -> 145 us
  Pallas kernels: 147 us -> 142 us
    pallas_call x1, Pallas kernels: 147 us -> 142 us  [per_device_fused(): pl.pallas_call(fused, out_shape=jax.ShapeDtypeStruct((tokens, width), bf1...]
where the time goes in v2:
time: 146 us; the launch traced here: 145 us
  Pallas kernels  142 us (97%)
  other arithmetic  2.15 us (1%)
    pallas_call x1, Pallas kernels, per_device_fused(): pl.pallas_call(fused, out_shape=jax.ShapeDtypeStruct((tokens, width), bf1...  142 us

profile of v2, /device:TPU:1, one launch (start us, length us, event | category | flops | bytes accessed | tf_op | source)
XLA Modules:
  0.0 145.3 jit_solution(16906231043982560662)
XLA Ops:
  1.3 141.8 %picard.1 = bf16[256,1152]{1,0:T(8,128)(2,1)} custom-call(s32[1]{0:T(128)S(6)} %copy.11.start_ref, s32[1]{0:T(128)S(6)} %copy.12.adv_ref, f32[1000]{0:T(1024)} %dt_ref.1, f32[1000]{0:T(1024)} %sg_ref.1, f32[1,1152]{1,0:T(1,128)} %cls_ref.1, f32[256,1152]{1,0:T(8,128)} %bitcast.5, bf16[2,256,1152]{2,1,0:T(8,128)(2,1)} %bitcast.6, bf16[144,1152]{1,0:T(8,128)(2,1)} %wup_ref.1, ...), custom_call_target="tpu_custom_call" | custom-call | flops 10871635968 | bytes 7962624 | tf_op jit(solution)/shard_map/picard/pallas_call | solution.py:519
  143.1 2.2 %bitcast_convert_fusion = f32[1,1,256,1152]{3,2,1,0:T(8,128)} fusion(bf16[256,1152]{1,0:T(8,128)(2,1)} %picard.1), kind=kLoop, calls=%fused_computation | loop fusion | flops 294912 | bytes 1769472 | tf_op jit(solution)/shard_map/broadcast_in_dim | solution.py:563

commit v3 on v2

--- a/solution.py
+++ b/solution.py
@@ -119,14 +119,15 @@
 
 
 SPLIT = (0, 2, 6, 9)
-TURNED = 2
+LATE = 2
+TURNED = 1
 
 
 def fused(
     start_ref, adv_ref, dt_ref, sg_ref, cls_ref, state_ref, noise_ref, wup_ref, wdn_ref, wada_ref,
     out_ref,
     up_full, dn_full, ada_buf, mod, a_send, a_recv, lo_send, lo_recv, cur, hid, acc, pre, o_send, act_all,
-    loc_sem, w_recv, z_sem, x_sem, y_sem, s_sem, a_ssem, a_rsem, n_ssem, n_rsem, l_ssem, l_rsem, o_ssem, o_rsem,
+    loc_sem, w_recv, z_sem, r_sem, x_sem, y_sem, s_sem, a_ssem, a_rsem, n_ssem, n_rsem, l_ssem, l_rsem, o_ssem, o_rsem,
 ):
     tokens, width = state_ref.shape
     part = tokens // WIN
@@ -150,18 +151,25 @@
     pl.semaphore_signal(barrier, inc=1, device_id=s_dev, device_id_type=MESH)
     pl.semaphore_wait(barrier, WIN + 1)
 
-    full = (up_full, dn_full)
-    given = (wup_ref, wdn_ref)
+    late = depth * LATE // 9 // 16 * 16
+    pieces = (
+        (wup_ref, up_full, 0, depth), (wdn_ref, dn_full, 0, depth - late), (wdn_ref, dn_full, depth - late, late),
+    )
 
     def block(w, sid):
-        return full[w].at[pl.ds(pl.multiple_of(sid * depth, 16), depth)]
+        _, full, lo, count = pieces[w]
+        return full.at[pl.ds(pl.multiple_of(sid * depth + lo, 16), count)]
+
+    def given(w):
+        ref, _, lo, count = pieces[w]
+        return ref.at[pl.ds(lo, count)]
 
     def ident(zz, xx, yy, cc):
         return (zz * 2 + xx) * 4 + yy * 2 + cc
 
     def send(w, sid, to, sem, own=False):
         pltpu.make_async_remote_copy(
-            src_ref=given[w] if own else block(w, sid), dst_ref=block(w, sid),
+            src_ref=given(w) if own else block(w, sid), dst_ref=block(w, sid),
             send_sem=sem, recv_sem=w_recv.at[w, sid], device_id=to, device_id_type=MESH,
         ).start()
 
@@ -172,7 +180,7 @@
         ).wait_recv()
 
     turned = depth * TURNED // 9 // 16 * 16
-    cuts = ((0, turned), (turned, depth - turned))
+    cuts = ((0, turned), (turned, depth - late - turned))
 
     def piece(k, sid):
         return dn_full.at[pl.ds(pl.multiple_of(sid * depth + cuts[k][0], 16), cuts[k][1])]
@@ -180,12 +188,12 @@
     def piece_copy(k, sid, to, sem):
         return pltpu.make_async_remote_copy(
             src_ref=piece(k, sid), dst_ref=piece(k, sid),
-            send_sem=sem, recv_sem=w_recv.at[1 + k, sid], device_id=to, device_id_type=MESH,
+            send_sem=sem, recv_sem=w_recv.at[1 + 2 * k, sid], device_id=to, device_id_type=MESH,
         )
 
     def sent(w, sem):
         pltpu.make_async_remote_copy(
-            src_ref=given[w], dst_ref=block(w, 0),
+            src_ref=given(w), dst_ref=block(w, 0),
             send_sem=sem, recv_sem=w_recv.at[w, 0], device_id=s_dev, device_id_type=MESH,
         ).wait_send()
 
@@ -210,6 +218,46 @@
             send(w, from_x, s_dev, s_sem.at[w, 1, zz])
             send(w, from_y, s_dev, s_sem.at[w, 2, zz])
 
+    def columns_of(zz):
+        return (ident(zz, x, y, c), ident(zz, xn, y, c), ident(zz, x, yn, c), ident(zz, xn, yn, c))
+
+    def late_on(zz, kind, up, down, own=False):
+        sid = columns_of(zz)[kind]
+        if up:
+            @pl.when(z < LAYERS - 1)
+            def _():
+                send(2, sid, up_dev, r_sem.at[0, kind, zz], own)
+        if down:
+            @pl.when(z > 0)
+            def _():
+                send(2, sid, down_dev, r_sem.at[1, kind, zz], own)
+        if not own:
+            send(2, sid, s_dev, s_sem.at[2, kind, zz])
+
+    def late_layer():
+        mine_, from_x, from_y, across = columns_of(z)
+        late_on(z, 0, True, True, True)
+        arrive(2, from_x)
+        send(2, from_x, y_dev, y_sem.at[2, 1, z])
+        late_on(z, 1, True, True)
+        arrive(2, from_y)
+        late_on(z, 2, True, True)
+        arrive(2, across)
+        late_on(z, 3, True, True)
+
+    def late_z(r):
+        @pl.when(z >= r)
+        def _():
+            for kind in range(4):
+                arrive(2, columns_of(z - r)[kind])
+                late_on(z - r, kind, True, False)
+
+        @pl.when(z + r < LAYERS)
+        def _():
+            for kind in range(4):
+                arrive(2, columns_of(z + r)[kind])
+                late_on(z + r, kind, False, True)
+
     me = ident(z, x, y, c)
 
     @pl.when(z < LAYERS - 1)
@@ -223,10 +271,14 @@
             send(w, me, down_dev, z_sem.at[w, 1, z], True)
 
     spread(z, True)
+    send(2, me, x_dev, x_sem.at[2, 0, z], True)
+    send(2, me, y_dev, y_sem.at[2, 0, z], True)
+    send(2, me, s_dev, s_sem.at[2, 0, z], True)
     local = [
         pltpu.make_async_copy(wada_ref, ada_buf, loc_sem.at[0]),
-        pltpu.make_async_copy(wup_ref, block(0, me), loc_sem.at[1]),
-        pltpu.make_async_copy(wdn_ref, block(1, me), loc_sem.at[2]),
+        pltpu.make_async_copy(given(0), block(0, me), loc_sem.at[1]),
+        pltpu.make_async_copy(given(1), block(1, me), loc_sem.at[2]),
+        pltpu.make_async_copy(given(2), block(2, me), loc_sem.at[3]),
     ]
     for copy in local:
         copy.start()
@@ -245,8 +297,8 @@
     row = lax.broadcasted_iota(jnp.int32, (2 * WIN, width), 0)
     lane = lax.broadcasted_iota(jnp.int32, (2 * WIN, width), 1)
     half = width // 2
-    late = row >= WIN
-    steps = (start + jnp.where(late, adv + row - WIN, row)).astype(jnp.float32)
+    second_sweep = row >= WIN
+    steps = (start + jnp.where(second_sweep, adv + row - WIN, row)).astype(jnp.float32)
     turn = jnp.where(lane >= half, lane - half, lane).astype(jnp.float32)
     angles = steps * jnp.exp(-math.log(10000.0) * turn / half)
     embed = jnp.where(lane >= half, jnp.sin(angles), jnp.cos(angles))
@@ -321,6 +373,7 @@
 
     round_z(1)
     round_side(0)
+    late_layer()
     round_z(2)
     for d in range(1, WIN):
         a_copy(d).start()
@@ -332,11 +385,10 @@
             l_copy(d).start()
 
     round_side(1)
+    late_z(1)
     round_z(3)
+    late_z(2)
     round_side(2)
-    round_side(3)
-    for d in range(1, WIN):
-        n_copy(d).start()
 
     def a_arrive(d):
         src = (tm + d) % WIN
@@ -351,16 +403,6 @@
             src_ref=a_send.at[src, second], dst_ref=a_recv.at[src, second], send_sem=n_ssem.at[d],
             recv_sem=n_rsem.at[src], device_id=(src, bt), device_id_type=MESH,
         ).wait_recv()
-
-    for d in range(1, WIN):
-        a_arrive(d)
-
-    @pl.when(tm > 0)
-    def _():
-        l_copy(1).wait_recv()
-
-    for j in range(WIN):
-        cur[j] = a_recv[j, 0:part, :].astype(jnp.float32)
 
     def before_mlp(s):
         @pl.loop(0, WIN)
@@ -392,12 +434,21 @@
             noise = a_recv[j, part : 2 * part, :].astype(jnp.float32)
             pre[j + 1] = pre[j] + (dt_ref[k] * (gate * acc[rows, :] - cur[j]) + sg_ref[k] * noise)
 
+    for d in range(1, WIN):
+        a_arrive(d)
+
+    @pl.when(tm > 0)
+    def _():
+        l_copy(1).wait_recv()
+
+    for j in range(WIN):
+        cur[j] = a_recv[j, 0:part, :].astype(jnp.float32)
+
     before_mlp(0)
     flip = z // 2
     near = z + flip * (3 - 2 * z)
 
-    @pl.loop(0, LAYERS)
-    def _(p):
+    def through(p):
         early = 1 - p // 2
         order = p + near * early * (1 - 2 * p)
         zz = order + flip * (3 - 2 * order)
@@ -409,13 +460,19 @@
             send(w, across, s_dev, s_sem.at[w, 3, zz])
         for xx in (0, 1):
             for yy in (0, 1):
-                for w in (0, 1):
+                for w in (0, 1, 2):
                     arrive(w, ident(zz, xx, yy, cn))
 
         @pl.loop(0, 3)
         def _(i):
             mlp(zz * layer + i * (layer // 3), layer // 3)
 
+    pl.loop(0, 2)(through)
+    late_z(3)
+    round_side(3)
+    for d in range(1, WIN):
+        n_copy(d).start()
+    pl.loop(2, LAYERS)(through)
     after_mlp(cur[0] + lo_recv[...].astype(jnp.float32))
     for j in range(WIN):
         cur[j] = pre[jnp.minimum(adv + j, WIN)]
@@ -473,6 +530,9 @@
     mine = pltpu.make_async_copy(o_send.at[tm], out_ref.at[own_rows], loc_sem.at[0])
     mine.start()
 
+    sent(2, x_sem.at[2, 0, z])
+    sent(2, y_sem.at[2, 0, z])
+    sent(2, y_sem.at[2, 1, z])
     for zz in range(LAYERS):
         for w in (0, 1):
             @pl.when((z < LAYERS - 1) & (zz <= z))
@@ -485,8 +545,18 @@
 
             sent(w, x_sem.at[w, 0, zz])
             sent(w, y_sem.at[w, 0, zz])
+        for w in (0, 1, 2):
             for kind in range(4):
                 sent(w, s_sem.at[w, kind, zz])
+        for kind in range(4):
+            @pl.when((z < LAYERS - 1) & (zz <= z))
+            def _():
+                sent(2, r_sem.at[0, kind, zz])
+
+            @pl.when((z > 0) & (zz >= z))
+            def _():
+                sent(2, r_sem.at[1, kind, zz])
+
         sent(0, y_sem.at[0, 1, zz])
         piece_copy(1, 0, s_dev, x_sem.at[1, 1, zz]).wait_send()
         piece_copy(0, 0, s_dev, y_sem.at[1, 1, zz]).wait_send()
@@ -536,12 +606,13 @@
             pltpu.VMEM((WIN + 1, part, width), f32),
             pltpu.VMEM((WIN, part, width), bf16),
             pltpu.VMEM(((WIN - 1) * part, hidden), bf16),
-            dma((3,)),
-            dma((3, 32)),
-            dma((2, 2, LAYERS)),
-            dma((2, 2, LAYERS)),
+            dma((4,)),
+            dma((4, 32)),
             dma((2, 2, LAYERS)),
             dma((2, 4, LAYERS)),
+            dma((3, 2, LAYERS)),
+            dma((3, 2, LAYERS)),
+            dma((3, 4, LAYERS)),
             dma((WIN,)),
             dma((WIN,)),
             dma((WIN,)),

time: 146 us -> 154 us (1.055)
  Pallas kernels: 142 us -> 150 us
    pallas_call x1, Pallas kernels: 142 us -> 150 us  [per_device_fused(): pl.pallas_call(fused, out_shape=jax.ShapeDtypeStruct((tokens, width), bf1...]
where the time goes in v3:
time: 154 us
  Pallas kernels  150 us (97%)
  other arithmetic  2.15 us (1%)
    pallas_call x1, Pallas kernels, per_device_fused(): pl.pallas_call(fused, out_shape=jax.ShapeDtypeStruct((tokens, width), bf1...  150 us

profile of v3, /device:TPU:1, one launch (start us, length us, event | category | flops | bytes accessed | tf_op | source)
XLA Modules:
  0.0 153.8 jit_solution(11408869598962431351)
XLA Ops:
  1.3 150.3 %picard.1 = bf16[256,1152]{1,0:T(8,128)(2,1)} custom-call(s32[1]{0:T(128)S(6)} %copy.11.start_ref, s32[1]{0:T(128)S(6)} %copy.12.adv_ref, f32[1000]{0:T(1024)} %dt_ref.1, f32[1000]{0:T(1024)} %sg_ref.1, f32[1,1152]{1,0:T(1,128)} %cls_ref.1, f32[256,1152]{1,0:T(8,128)} %bitcast.5, bf16[2,256,1152]{2,1,0:T(8,128)(2,1)} %bitcast.6, bf16[144,1152]{1,0:T(8,128)(2,1)} %wup_ref.1, ...), custom_call_target="tpu_custom_call" | custom-call | flops 10871635968 | bytes 7962624 | tf_op jit(solution)/shard_map/picard/pallas_call | solution.py:589
  151.6 2.2 %bitcast_convert_fusion = f32[1,1,256,1152]{3,2,1,0:T(8,128)} fusion(bf16[256,1152]{1,0:T(8,128)(2,1)} %picard.1), kind=kLoop, calls=%fused_computation | loop fusion | flops 294912 | bytes 1769472 | tf_op jit(solution)/shard_map/broadcast_in_dim | solution.py:634

commit v4 on v2

--- a/solution.py
+++ b/solution.py
@@ -375,12 +375,15 @@
             hid[rows, :] = (normed * (1.0 + scale) + shift).astype(jnp.bfloat16)
             acc[rows, :] = jnp.zeros((part, width), jnp.float32)
 
-    def mlp(first, count):
+    def activations(first, count):
         rows = pl.ds(pl.multiple_of(first, 128), count)
         before = lax.dot_general(
-            hid[...], up_full[rows, :], (((1,), (1,)), ((), ())), preferred_element_type=jnp.float32
-        )
-        act = jax.nn.gelu(before, approximate=True).astype(jnp.bfloat16)
+            up_full[rows, :], hid[...], (((1,), (1,)), ((), ())), preferred_element_type=jnp.float32
+        )
+        return rows, jax.nn.gelu(before, approximate=True).astype(jnp.bfloat16).T
+
+    def mlp(first, count):
+        rows, act = activations(first, count)
         acc[...] += jnp.dot(act, dn_full[rows, :], preferred_element_type=jnp.float32)
 
     def after_mlp(base):
@@ -412,26 +415,18 @@
                 for w in (0, 1):
                     arrive(w, ident(zz, xx, yy, cn))
 
-        @pl.loop(0, 3)
-        def _(i):
-            mlp(zz * layer + i * (layer // 3), layer // 3)
+        mlp(zz * layer, layer)
 
     after_mlp(cur[0] + lo_recv[...].astype(jnp.float32))
     for j in range(WIN):
         cur[j] = pre[jnp.minimum(adv + j, WIN)]
     before_mlp(1)
     rows_used = (WIN - 1) * part
-    hidden = LAYERS * layer
-
-    @pl.loop(0, 3)
+
+    @pl.loop(0, LAYERS)
     def _(i):
-        for k in range(3):
-            rows = pl.ds(pl.multiple_of((i * 3 + k) * (hidden // 9), 128), hidden // 9)
-            before = lax.dot_general(
-                hid[0:rows_used, :], up_full[rows, :], (((1,), (1,)), ((), ())),
-                preferred_element_type=jnp.float32,
-            )
-            act_all[:, rows] = jax.nn.gelu(before, approximate=True).astype(jnp.bfloat16)
+        rows, act = activations(i * layer, layer)
+        act_all[:, rows] = act
 
     own_rows = pl.ds(pl.multiple_of(tm * part, part), part)
 
@@ -457,7 +452,7 @@
     edges = tuple(width * e // 9 for e in SPLIT)
     spans = tuple(pl.ds(lo, hi - lo) for lo, hi in zip(edges, edges[1:]))
     for b, (lo, hi) in enumerate(zip(edges, edges[1:])):
-        mlp_out = jnp.dot(act_all[...], dn_full[:, lo:hi], preferred_element_type=jnp.float32)
+        mlp_out = jnp.dot(act_all[0:rows_used, :], dn_full[:, lo:hi], preferred_element_type=jnp.float32)
         total = cur[0, :, lo:hi]
         for j in range(WIN):
             o_send[j, :, lo:hi] = total.astype(jnp.bfloat16)
@@ -535,7 +530,7 @@
             pltpu.VMEM((tokens, width), f32),
             pltpu.VMEM((WIN + 1, part, width), f32),
             pltpu.VMEM((WIN, part, width), bf16),
-            pltpu.VMEM(((WIN - 1) * part, hidden), bf16),
+            pltpu.VMEM((tokens, hidden), bf16),
             dma((3,)),
             dma((3, 32)),
             dma((2, 2, LAYERS)),

time: 146 us -> 147 us (level)
  Pallas kernels: 142 us -> 144 us
    pallas_call x1, Pallas kernels: 142 us -> 144 us  [per_device_fused(): pl.pallas_call(fused, out_shape=jax.ShapeDtypeStruct((tokens, width), bf1...]
where the time goes in v4:
time: 147 us
  Pallas kernels  144 us (98%)
  other arithmetic  2.15 us (1%)
    pallas_call x1, Pallas kernels, per_device_fused(): pl.pallas_call(fused, out_shape=jax.ShapeDtypeStruct((tokens, width), bf1...  144 us

profile of v4, /device:TPU:1, one launch (start us, length us, event | category | flops | bytes accessed | tf_op | source)
XLA Modules:
  0.0 147.1 jit_solution(10150060530911983980)
XLA Ops:
  1.3 143.6 %picard.1 = bf16[256,1152]{1,0:T(8,128)(2,1)} custom-call(s32[1]{0:T(128)S(6)} %copy.11.start_ref, s32[1]{0:T(128)S(6)} %copy.12.adv_ref, f32[1000]{0:T(1024)} %dt_ref.1, f32[1000]{0:T(1024)} %sg_ref.1, f32[1,1152]{1,0:T(1,128)} %cls_ref.1, f32[256,1152]{1,0:T(8,128)} %bitcast.5, bf16[2,256,1152]{2,1,0:T(8,128)(2,1)} %bitcast.6, bf16[144,1152]{1,0:T(8,128)(2,1)} %wup_ref.1, ...), custom_call_target="tpu_custom_call" | custom-call | flops 10871635968 | bytes 7962624 | tf_op jit(solution)/shard_map/picard/pallas_call | solution.py:514
  144.9 2.2 %bitcast_convert_fusion = f32[1,1,256,1152]{3,2,1,0:T(8,128)} fusion(bf16[256,1152]{1,0:T(8,128)(2,1)} %picard.1), kind=kLoop, calls=%fused_computation | loop fusion | flops 294912 | bytes 1769472 | tf_op jit(solution)/shard_map/broadcast_in_dim | solution.py:558

commit v5 on v2

--- a/solution.py
+++ b/solution.py
@@ -334,9 +334,6 @@
     round_side(1)
     round_z(3)
     round_side(2)
-    round_side(3)
-    for d in range(1, WIN):
-        n_copy(d).start()
 
     def a_arrive(d):
         src = (tm + d) % WIN
@@ -396,8 +393,7 @@
     flip = z // 2
     near = z + flip * (3 - 2 * z)
 
-    @pl.loop(0, LAYERS)
-    def _(p):
+    def through(p):
         early = 1 - p // 2
         order = p + near * early * (1 - 2 * p)
         zz = order + flip * (3 - 2 * order)
@@ -416,6 +412,11 @@
         def _(i):
             mlp(zz * layer + i * (layer // 3), layer // 3)
 
+    pl.loop(0, 2)(through)
+    round_side(3)
+    for d in range(1, WIN):
+        n_copy(d).start()
+    pl.loop(2, LAYERS)(through)
     after_mlp(cur[0] + lo_recv[...].astype(jnp.float32))
     for j in range(WIN):
         cur[j] = pre[jnp.minimum(adv + j, WIN)]

time: 146 us -> 141 us (0.966)
  Pallas kernels: 142 us -> 137 us
    pallas_call x1, Pallas kernels: 142 us -> 137 us  [per_device_fused(): pl.pallas_call(fused, out_shape=jax.ShapeDtypeStruct((tokens, width), bf1...]
where the time goes in v5:
time: 141 us; the launch traced here: 140 us
  Pallas kernels  137 us (97%)
  other arithmetic  2.15 us (2%)
    pallas_call x1, Pallas kernels, per_device_fused(): pl.pallas_call(fused, out_shape=jax.ShapeDtypeStruct((tokens, width), bf1...  137 us

profile of v5, /device:TPU:1, one launch (start us, length us, event | category | flops | bytes accessed | tf_op | source)
XLA Modules:
  0.0 140.3 jit_solution(1267732403837996303)
XLA Ops:
  1.3 136.8 %picard.1 = bf16[256,1152]{1,0:T(8,128)(2,1)} custom-call(s32[1]{0:T(128)S(6)} %copy.11.start_ref, s32[1]{0:T(128)S(6)} %copy.12.adv_ref, f32[1000]{0:T(1024)} %dt_ref.1, f32[1000]{0:T(1024)} %sg_ref.1, f32[1,1152]{1,0:T(1,128)} %cls_ref.1, f32[256,1152]{1,0:T(8,128)} %bitcast.5, bf16[2,256,1152]{2,1,0:T(8,128)(2,1)} %bitcast.6, bf16[144,1152]{1,0:T(8,128)(2,1)} %wup_ref.1, ...), custom_call_target="tpu_custom_call" | custom-call | flops 10871635968 | bytes 7962624 | tf_op jit(solution)/shard_map/picard/pallas_call | solution.py:520
  138.1 2.2 %bitcast_convert_fusion = f32[1,1,256,1152]{3,2,1,0:T(8,128)} fusion(bf16[256,1152]{1,0:T(8,128)(2,1)} %picard.1), kind=kLoop, calls=%fused_computation | loop fusion | flops 294912 | bytes 1769472 | tf_op jit(solution)/shard_map/broadcast_in_dim | solution.py:564

commit v6 on v5

--- a/solution.py
+++ b/solution.py
@@ -257,7 +257,7 @@
         columns = slice(third * width, (third + 1) * width)
         mod[:, columns] = jnp.dot(condition, ada_buf[:, columns], preferred_element_type=jnp.float32)
 
-    first, second = pl.ds(0, 2 * part), pl.ds(2 * part, part)
+    first, spans_n = pl.ds(0, part), (pl.ds(part, part), pl.ds(2 * part, part))
 
     def a_copy(d):
         to = (tm + d) % WIN
@@ -266,11 +266,11 @@
             recv_sem=a_rsem.at[tm], device_id=(to, bt), device_id_type=MESH,
         )
 
-    def n_copy(d):
+    def n_copy(s, d):
         to = (tm + d) % WIN
         return pltpu.make_async_remote_copy(
-            src_ref=a_send.at[to, second], dst_ref=a_recv.at[tm, second], send_sem=n_ssem.at[d],
-            recv_sem=n_rsem.at[tm], device_id=(to, bt), device_id_type=MESH,
+            src_ref=a_send.at[to, spans_n[s]], dst_ref=a_recv.at[tm, spans_n[s]], send_sem=n_ssem.at[s, d],
+            recv_sem=n_rsem.at[s, tm], device_id=(to, bt), device_id_type=MESH,
         )
 
     def l_copy(d):
@@ -342,13 +342,15 @@
             recv_sem=a_rsem.at[src], device_id=(src, bt), device_id_type=MESH,
         ).wait_recv()
 
-    def n_arrive(d):
+    def n_arrive(s, d):
         src = (tm + d) % WIN
         pltpu.make_async_remote_copy(
-            src_ref=a_send.at[src, second], dst_ref=a_recv.at[src, second], send_sem=n_ssem.at[d],
-            recv_sem=n_rsem.at[src], device_id=(src, bt), device_id_type=MESH,
+            src_ref=a_send.at[src, spans_n[s]], dst_ref=a_recv.at[src, spans_n[s]], send_sem=n_ssem.at[s, d],
+            recv_sem=n_rsem.at[s, src], device_id=(src, bt), device_id_type=MESH,
         ).wait_recv()
 
+    for d in range(1, WIN):
+        n_copy(0, d).start()
     for d in range(1, WIN):
         a_arrive(d)
 
@@ -415,8 +417,10 @@
     pl.loop(0, 2)(through)
     round_side(3)
     for d in range(1, WIN):
-        n_copy(d).start()
+        n_copy(1, d).start()
     pl.loop(2, LAYERS)(through)
+    for d in range(1, WIN):
+        n_arrive(0, d)
     after_mlp(cur[0] + lo_recv[...].astype(jnp.float32))
     for j in range(WIN):
         cur[j] = pre[jnp.minimum(adv + j, WIN)]
@@ -454,7 +458,7 @@
         ).wait_recv()
 
     for d in range(1, WIN):
-        n_arrive(d)
+        n_arrive(1, d)
     edges = tuple(width * e // 9 for e in SPLIT)
     spans = tuple(pl.ds(lo, hi - lo) for lo, hi in zip(edges, edges[1:]))
     for b, (lo, hi) in enumerate(zip(edges, edges[1:])):
@@ -493,7 +497,8 @@
         piece_copy(0, 0, s_dev, y_sem.at[1, 1, zz]).wait_send()
     for d in range(1, WIN):
         a_copy(d).wait_send()
-        n_copy(d).wait_send()
+        n_copy(0, d).wait_send()
+        n_copy(1, d).wait_send()
 
     @pl.when(tm == 0)
     def _():
@@ -545,8 +550,8 @@
             dma((2, 4, LAYERS)),
             dma((WIN,)),
             dma((WIN,)),
-            dma((WIN,)),
-            dma((WIN,)),
+            dma((2, WIN)),
+            dma((2, WIN)),
             dma((WIN,)),
             dma,
             dma((len(SPLIT) - 1, WIN)),

time: 141 us -> 141 us (level)
  no operation moved by 1% of the time
where the time goes in v6:
time: 141 us; the launch traced here: 140 us
  Pallas kernels  137 us (97%)
  other arithmetic  2.15 us (2%)
    pallas_call x1, Pallas kernels, per_device_fused(): pl.pallas_call(fused, out_shape=jax.ShapeDtypeStruct((tokens, width), bf1...  137 us

profile of v6, /device:TPU:1, one launch (start us, length us, event | category | flops | bytes accessed | tf_op | source)
XLA Modules:
  0.0 140.3 jit_solution(3790805568236552032)
XLA Ops:
  1.3 136.8 %picard.1 = bf16[256,1152]{1,0:T(8,128)(2,1)} custom-call(s32[1]{0:T(128)S(6)} %copy.11.start_ref, s32[1]{0:T(128)S(6)} %copy.12.adv_ref, f32[1000]{0:T(1024)} %dt_ref.1, f32[1000]{0:T(1024)} %sg_ref.1, f32[1,1152]{1,0:T(1,128)} %cls_ref.1, f32[256,1152]{1,0:T(8,128)} %bitcast.5, bf16[2,256,1152]{2,1,0:T(8,128)(2,1)} %bitcast.6, bf16[144,1152]{1,0:T(8,128)(2,1)} %wup_ref.1, ...), custom_call_target="tpu_custom_call" | custom-call | flops 10871635968 | bytes 7962624 | tf_op jit(solution)/shard_map/picard/pallas_call | solution.py:525
  138.1 2.2 %bitcast_convert_fusion = f32[1,1,256,1152]{3,2,1,0:T(8,128)} fusion(bf16[256,1152]{1,0:T(8,128)(2,1)} %picard.1), kind=kLoop, calls=%fused_computation | loop fusion | flops 294912 | bytes 1769472 | tf_op jit(solution)/shard_map/broadcast_in_dim | solution.py:569
